TPU v7x, 512 devices: a whole 4x4x16 slice. The times are simulated.
512 devices in a mesh: dp: 8 (over y, core), expert: 16 (over z), tensor: 4 (over x).
Axes of the slice: x: 4, y: 4, z: 16, core: 2. Of those that a mesh axis runs over, the one named last changes fastest.
Arguments:
- grad_out: bfloat16 [16384, 4096], P(('dp', 'expert'), 'tensor'), may hold values from -6 to 6
- tokens_in: bfloat16 [16384, 4096], P(('dp', 'expert'), 'tensor'), may hold values from -6 to 6
- router_logits: float32 [16384, 16], P(('dp', 'expert')), may hold values from -8 to 8
- expert_ids: int32 [16384, 2], P(('dp', 'expert')), may hold values from 0 to 15, as said below
- slot_index: int32 [16384, 2], P(('dp', 'expert')), may hold values from 0 to 7, as said below
- kept: int32 [16384, 2], P(('dp', 'expert')), may hold values from 0 to 1, as said below
- expert_out: bfloat16 [16384, 2, 4096], P(('dp', 'expert'), None, 'tensor'), may hold values from -0.0234375 to 0.0234375
- gate_pre: bfloat16 [16, 1024, 7168], P('expert', None, ('dp', 'tensor')), may hold values from -6 to 6
- up_pre: bfloat16 [16, 1024, 7168], P('expert', None, ('dp', 'tensor')), may hold values from -6 to 6
- down_weight: bfloat16 [16, 7168, 4096], P('expert', ('dp', 'tensor')), may hold values from -0.0625 to 0.0625
Outputs:
- gate_grad: bfloat16 [16, 1024, 7168], P('expert', None, ('dp', 'tensor'))
- up_grad: bfloat16 [16, 1024, 7168], P('expert', None, ('dp', 'tensor'))
- router_grad: float32 [16, 4096], P(None, 'tensor')
Inputs may be any that keep to these rules, and one draw needn't show every extreme that they name: `expert_ids`: the two experts of a token differ. `slot_index`: for a kept route, the number of earlier routes of its group of 128 tokens to the same expert, tokens in order and a token's first route before its second; 0 for a dropped route. `kept`: 1 exactly where that number of earlier routes is below 8.
All inputs are finite; a program needn't handle non-finite values.
Results may differ from a plain program's by a relative error of at most 0.0049.
Values may be sent and summed in bfloat16 or wider, within the bound.
A program may use at most 64 MiB of HBM per device.

v0:
```python
import jax
import jax.numpy as jnp
from jax import lax
from jax.sharding import PartitionSpec as P

TOP = 2


def body(
    grad_out,
    tokens_in,
    router_logits,
    expert_ids,
    slot_index,
    kept,
    expert_out,
    gate_pre,
    up_pre,
    down_weight,
):
    experts = router_logits.shape[1]
    tensor_count = lax.axis_size("tensor")
    tensor_pos = lax.axis_index("tensor")
    tok_rows = grad_out.shape[0]
    capacity = tok_rows * TOP // (2 * experts)
    per_member = capacity // tensor_count
    full_grad = lax.all_gather(grad_out, "tensor", axis=1, tiled=True)
    model_width = full_grad.shape[1]
    onehot = (expert_ids[:, :, None] == jnp.arange(experts, dtype=jnp.int32)[None, None, :]).astype(
        jnp.float32
    )
    chosen = jnp.sum(onehot * router_logits[:, None, :], axis=2)
    prob_first = jax.nn.sigmoid(chosen[:, 0] - chosen[:, 1])
    prob_second = 1.0 - prob_first
    weights = jnp.stack([prob_first, prob_second], axis=1)
    keep_float = kept.astype(jnp.float32)
    is_mine = jnp.logical_and(slot_index // per_member == tensor_pos, kept == 1)
    target = expert_ids * per_member + slot_index % per_member
    select = jnp.logical_and(
        target.reshape(-1)[None, :] == jnp.arange(experts * per_member, dtype=jnp.int32)[:, None],
        is_mine.reshape(-1)[None, :],
    )
    scaled = (
        (weights * keep_float)[:, :, None] * full_grad.astype(jnp.float32)[:, None, :]
    ).astype(jnp.bfloat16)
    outgoing = jnp.dot(
        select.astype(jnp.bfloat16),
        scaled.reshape(tok_rows * TOP, model_width),
        preferred_element_type=jnp.float32,
    )
    outgoing = outgoing.astype(jnp.bfloat16).reshape(experts, per_member, model_width)
    received = lax.all_to_all(outgoing, "expert", split_axis=0, concat_axis=0, tiled=True).reshape(
        experts * per_member, model_width
    )
    down_rows = down_weight[0]
    hidden_grad = lax.dot_general(
        lax.all_gather(received, ("dp", "tensor"), axis=0, tiled=True),
        down_rows,
        (((1,), (1,)), ((), ())),
        preferred_element_type=jnp.float32,
    )
    gate_vals = gate_pre[0].astype(jnp.float32)
    sigma_gate = jax.nn.sigmoid(gate_vals)
    up_grad = (hidden_grad * gate_vals * sigma_gate).astype(jnp.bfloat16)
    gate_grad = (
        hidden_grad
        * up_pre[0].astype(jnp.float32)
        * sigma_gate
        * (1.0 + gate_vals * (1.0 - sigma_gate))
    ).astype(jnp.bfloat16)
    partial_scores = jnp.sum(
        grad_out.astype(jnp.float32)[:, None, :] * expert_out.astype(jnp.float32), axis=2
    )
    scores = lax.psum(partial_scores, "tensor") * keep_float
    coefficient = prob_first * prob_second * (scores[:, 0] - scores[:, 1])
    logit_grad = coefficient[:, None] * (onehot[:, 0, :] - onehot[:, 1, :])
    router_term = jnp.dot(
        logit_grad.T, tokens_in.astype(jnp.float32), precision=lax.Precision.HIGHEST
    )
    router_grad = lax.psum(router_term, ("dp", "expert"))
    return (gate_grad[None], up_grad[None], router_grad)


def solution(mesh):
    in_specs = (
        P(("dp", "expert"), "tensor"),
        P(("dp", "expert"), "tensor"),
        P(("dp", "expert"), None),
        P(("dp", "expert"), None),
        P(("dp", "expert"), None),
        P(("dp", "expert"), None),
        P(("dp", "expert"), None, "tensor"),
        P("expert", None, ("dp", "tensor")),
        P("expert", None, ("dp", "tensor")),
        P("expert", ("dp", "tensor"), None),
    )
    out_specs = (
        P("expert", None, ("dp", "tensor")),
        P("expert", None, ("dp", "tensor")),
        P(None, "tensor"),
    )
    return jax.shard_map(body, mesh=mesh, in_specs=in_specs, out_specs=out_specs, check_vma=False)
```

profile of v0, /device:TPU:1, one launch (start us, length us, event | category | flops | bytes accessed | tf_op | source)
XLA Modules:
  0.0 411.0 jit_solution(11561525415720258712)
XLA Ops:
  8.0 0.0 all-gather.3.cloned.1.call-start
  8.1 0.7 all-gather.3.cloned.1.call-update
  8.7 0.0 all-gather.5.cloned.1.call-start
  8.8 1.0 convert_element_type.52
  9.8 1.7 multiply_reduce_fusion
  11.5 0.1 copy.44
  11.5 9.3 %psum.14 = f32[128,2]{0,1:T(2,128)S(1)} all-reduce(f32[128,2]{0,1:T(2,128)S(1)} %copy.44), channel_id=1, replica_groups=mesh['dp'=8,'expert'=16,'tensor'=4] {'tensor'}, use_global_device_ids=true, to_apply=%region_2.3 | all-reduce | flops 256 | bytes 2048 | tf_op jit(solution)/shard_map/psum | solution.py:74
  20.8 0.7 select_reduce_fusion
  21.5 0.7 convert_multiply_fusion.3
  22.2 0.7 maximum_multiply_fusion
  22.9 0.1 copy.43
  23.0 0.1 mul.87
  23.2 0.7 fusion.25
  23.9 0.1 copy.41
  24.0 0.1 eq.40
  24.2 0.7 compare_and_fusion
  24.9 0.1 copy.42
  25.0 0.1 and.27
  25.2 21.8 %all-gather.3.cloned.1.call-done = bf16[128,4096]{1,0:T(8,128)(2,1)} async-done(((bf16[128,1024]{1,0:T(8,128)(2,1)}), bf16[128,4096]{1,0:T(8,128)(2,1)}) %all-gather.3.cloned.1.call-update) | async-done | bytes 1048592 | tf_op jit(solution)/shard_map/all_gather | solution.py:27
  47.0 5.3 %mul.89 = f32[128,2,4096]{2,1,0:T(2,128)} broadcast(bf16[128,4096]{1,0:T(8,128)(2,1)} %all-gather.3.cloned.1.call-done), dimensions={0,2} | broadcast | bytes 5242880 | tf_op jit(solution)/shard_map/mul | solution.py:44
  52.3 6.1 %mul.90 = f32[256,4096]{1,0:T(8,128)} reshape(f32[128,2,4096]{2,1,0:T(2,128)} %mul.89) | data formatting | bytes 8388608 | tf_op jit(solution)/shard_map/mul | solution.py:44
  58.4 2.7 convolution_convert_fusion
  61.1 0.2 reshape.28
  61.3 24.6 %all_to_all.5 = bf16[16,2,4096]{2,1,0:T(2,128)(2,1)S(1)} all-to-all(bf16[16,2,4096]{2,1,0:T(2,128)(2,1)S(1)} %reshape.28), channel_id=1, replica_groups=mesh['dp'=8,'expert'=16,'tensor'=4] {'expert'}, dimensions={0} | all-to-all | bytes 524288 | tf_op jit(solution)/shard_map/all_to_all | solution.py:52
  85.9 0.8 reshape.29
  86.7 0.0 all-reduce.2.cloned.1.call-start
  86.8 0.9 fusion.21
  87.7 0.0 all-reduce.2.cloned.1.call-update
  87.7 67.7 %all-gather.5.cloned.1.call-done = bf16[1024,4096]{1,0:T(8,128)(2,1)} async-done(((bf16[32,4096]{1,0:T(8,128)(2,1)}), bf16[1024,4096]{1,0:T(8,128)(2,1)}) %all-gather.5.cloned.1.call-update) | async-done | bytes 8388624 | tf_op jit(solution)/shard_map/all_gather | solution.py:57
  155.4 7.3 %fusion.12 = (bf16[1,1024,224]{1,2,0:T(8,128)(2,1)}, bf16[1,1024,224]{1,2,0:T(8,128)(2,1)}) fusion(bf16[1,1024,224]{1,2,0:T(8,128)(2,1)S(1)} %copy-done.3, bf16[1,1024,224]{1,2,0:T(8,128)(2,1)} %param.18, bf16[1024,4096]{1,0:T(8,128)(2,1)} %all-gather.5.cloned.1.call-done, bf16[1,224,4096]{2,1,0:T(8,128)(2,1)S(1)} %copy-done), kind=kOutput, calls=%fused_computation.19 | convolution fusion | flops 1882488832 | bytes 12058624 | tf_op jit(solution)/shard_map/dot_general | solution.py:56
  162.8 239.3 %all-reduce.2.cloned.1.call-done = f32[16,1024]{1,0:T(8,128)} async-done(((f32[16,1024]{1,0:T(8,128)}), f32[16,1024]{1,0:T(8,128)}) %all-reduce.2.cloned.1.call-update) | async-done | bytes 65552 | tf_op jit(solution)/shard_map/psum | solution.py:80
  402.0 1.5 copy.46
  (12 shorter events, 0.1 us)
Async XLA Ops:
  8.0 147.4 %copy-start = (bf16[1,224,4096]{2,1,0:T(8,128)(2,1)S(1)}, bf16[1,224,4096]{2,1,0:T(8,128)(2,1)}, u32[]{:S(2)}) copy-start(bf16[1,224,4096]{2,1,0:T(8,128)(2,1)} %param.19) | copy-start | bytes 5505028
  8.0 39.0 %all-gather.3.cloned.1.call-start = ((), (), s32[]{:S(2)}) async-start(), calls=%async_computation.1 | async-start | bytes 1310720 | tf_op jit(solution)/shard_map/all_gather | solution.py:27
  8.7 146.7 %all-gather.5.cloned.1.call-start = ((), (), s32[]{:S(2)}) async-start(), calls=%async_computation.2 | async-start | bytes 8650752 | tf_op jit(solution)/shard_map/all_gather | solution.py:57
  58.4 28.4 %copy-start.2 = (s32[128,2]{0,1:T(2,128)S(1)}, s32[128,2]{0,1:T(2,128)}, u32[]{:S(2)}) copy-start(s32[128,2]{0,1:T(2,128)} %param.13) | copy-start | bytes 3076
  58.4 28.5 %copy-start.1 = (bf16[128,1024]{1,0:T(8,128)(2,1)S(1)}, bf16[128,1024]{1,0:T(8,128)(2,1)}, u32[]{:S(2)}) copy-start(bf16[128,1024]{1,0:T(8,128)(2,1)} %param.11) | copy-start | bytes 786436
  58.4 97.1 %copy-start.3 = (bf16[1,1024,224]{1,2,0:T(8,128)(2,1)S(1)}, bf16[1,1024,224]{1,2,0:T(8,128)(2,1)}, u32[]{:S(2)}) copy-start(bf16[1,1024,224]{1,2,0:T(8,128)(2,1)} %param.17) | copy-start | bytes 1376260
  86.7 315.3 %all-reduce.2.cloned.1.call-start = ((), (), s32[]{:S(2)}) async-start(), calls=%async_computation.3 | async-start | bytes 131072 | tf_op jit(solution)/shard_map/psum | solution.py:80
Sparse Core Ops, SparseCore 0:
  10.9 36.0 all-gather.2
  86.8 68.5 all-gather.4
Sparse Core Ops, SparseCore 1:
  91.2 310.8 all-reduce.1
where the time goes:
time: 411 us
  waiting for transfers between devices  330 us (80%)
  blocking collectives  33.9 us (8%)
  between operations  15.6 us (4%)
  local copies, waits for them, and re-layouts  14.7 us (4%)
  matrix products  10.9 us (3%)
  other arithmetic  6.2 us (2%)
    psum x1, waiting for transfers between devices, body(): router_grad = lax.psum(router_term, ('dp', 'expert'))  239 us
    all_gather x1, waiting for transfers between devices, body(): lax.all_gather(received, ('dp', 'tensor'), axis=0, tiled=True)  67.7 us
    all_to_all x1, blocking collectives, body(): lax.all_to_all(outgoing, 'expert', split_axis=0, concat_axis=0, tiled=True)  24.6 us
    all_gather x1, waiting for transfers between devices, body(): full_grad = lax.all_gather(grad_out, 'tensor', axis=1, tiled=True)  21.8 us
    mul x3, local copies, waits for them, and re-layouts, body(): (weights * keep_float)[:, :, None]  11.5 us
    psum x1, blocking collectives, body(): scores = lax.psum(partial_scores, 'tensor') * keep_float  9.29 us
  transfers between devices with their start and end apart: 3, of which 3 were waited for; matrix products, arithmetic and copies ran while one was open for 4% of the time, Pallas kernels for 0%

commit v1 on v0

v1 whole, which is shorter than its diff:
```python
import functools

import jax
import jax.numpy as jnp
from jax import lax
from jax.experimental import pallas as pl
from jax.experimental.pallas import tpu as pltpu
from jax.sharding import PartitionSpec as P

MESH = pl.DeviceIdType.MESH
F32 = jnp.float32
BF16 = jnp.bfloat16

NZ = 16
NX = 4
NY = 4
NJ = 2
HID = 224
HALF = 512
ROWS = 64

OWN, MINUS, PLUS, OPP = 0, 1, 2, 3


def kernel(
    g_hbm, tok_hbm, eo_hbm, gate_hbm, up_hbm, w_hbm, logits_ref, ids_ref, slot_ref, kept_ref,
    gg_hbm, ug_hbm, rg_ref,
    g, tok, eo, gate, up, wbuf, fac_u, fac_g, out_u, out_g,
    tx, rx_same, rx_cross, rows, p_own, p_tx, p_rx,
    sc_tx, sc_rx, rt, r1, r2, r3,
    in_sem, w_sem, wr_sem, z_send, z_recv, a_send, a_recv, p_send, p_recv,
    sc_send, sc_recv, r_send, r_recv, o_sem,
):
    dp = lax.axis_index("dp")
    z = lax.axis_index("expert")
    x = lax.axis_index("tensor")
    y = dp // 2
    c = dp % 2
    partner = dp + 1 - 2 * c
    xs = [x, (x + 3) % 4, (x + 1) % 4, (x + 2) % 4]
    ys = [y, (y + 3) % 4, (y + 1) % 4, (y + 2) % 4]

    def fetch(i, src, dst):
        copy = pltpu.make_async_copy(src, dst, in_sem.at[i])
        copy.start()
        return copy

    cp_g = fetch(0, g_hbm, g)
    cp_eo = fetch(1, eo_hbm, eo)
    cp_tok = fetch(2, tok_hbm, tok)
    cp_gate = fetch(3, gate_hbm.at[0], gate)
    cp_up = fetch(4, up_hbm.at[0], up)
    for q in range(NX):
        pltpu.make_async_copy(
            w_hbm.at[0, :, pl.ds(pl.multiple_of(q * 1024 + c * HALF, HALF), HALF)],
            wbuf.at[0, q],
            w_sem.at[0],
        ).start()

    barrier = pltpu.get_barrier_semaphore()

    def greet(**where):
        pl.semaphore_signal(barrier, inc=1, device_id=where, device_id_type=MESH)

    for k in range(1, NZ):
        greet(expert=(z + k) % NZ)
        greet(expert=(z + k) % NZ, dp=partner)
    for k in range(1, NX):
        greet(tensor=(x + k) % NX)
    for k in range(1, 2 * NY):
        greet(dp=(dp + k) % (2 * NY))

    ids = ids_ref[...]
    slots = slot_ref[...]
    kept = kept_ref[...]
    logits = logits_ref[...]
    expert_row = lax.broadcasted_iota(jnp.int32, (16, 128), 0)
    hot = [(expert_row == ids[k : k + 1, :]).astype(F32) for k in range(2)]
    chosen = [jnp.sum(hot[k] * logits, axis=0, keepdims=True) for k in range(2)]
    w0 = 1.0 / (1.0 + jnp.exp(chosen[1] - chosen[0]))
    wts = [w0, 1.0 - w0]
    keep = [kept[k : k + 1, :].astype(F32) for k in range(2)]

    row = lax.broadcasted_iota(jnp.int32, (256, 128), 0)
    row_key = (row // 16) * 4 + row % 4
    row_blk = (row // 4) % 4
    sel = []
    for j in range(NJ):
        one = jnp.zeros((256, 128), F32)
        val = jnp.zeros((256, 128), F32)
        for k in range(2):
            s = slots[k : k + 1, :]
            mine = jnp.logical_and(kept[k : k + 1, :] == 1, s // 4 == j)
            key = jnp.where(mine, ids[k : k + 1, :] * 4 + s % 4, -1)
            hit = (row_key == key).astype(F32)
            one = one + hit
            val = val + hit * wts[k]
        scale = jnp.sum(val, axis=1, keepdims=True)
        wide = jnp.concatenate(
            [jnp.where(row_blk == f, one, 0.0).astype(BF16) for f in range(4)], axis=1
        )
        sel.append((wide, scale))
    cp_g.wait()
    for h in range(2):
        tall = jnp.concatenate(
            [g[:, h * HALF + f * 128 : h * HALF + (f + 1) * 128] for f in range(4)], axis=0
        )
        for j in range(NJ):
            wide, scale = sel[j]
            picked = jnp.dot(wide, tall, preferred_element_type=F32)
            tx[j, h * NZ : (h + 1) * NZ] = (picked * scale).astype(BF16).reshape(NZ, 16, 128)

    pl.semaphore_wait(barrier, 2 * (NZ - 1) + (NX - 1) + (2 * NY - 1))

    order = []
    for k in range(1, NZ // 2):
        order += [k, NZ - k]
    order.append(NZ // 2)
    for j in range(NJ):
        for k in [0] + order:
            to = (z + k) % NZ
            pltpu.make_async_remote_copy(
                src_ref=tx.at[j, (1 - c) * NZ + to],
                dst_ref=rx_cross.at[j, k],
                send_sem=z_send.at[j],
                recv_sem=z_recv.at[j, 1],
                device_id={"expert": to, "dp": partner},
                device_id_type=MESH,
            ).start()
            if k > 0:
                pltpu.make_async_remote_copy(
                    src_ref=tx.at[j, c * NZ + to],
                    dst_ref=rx_same.at[j, k],
                    send_sem=z_send.at[j],
                    recv_sem=z_recv.at[j, 0],
                    device_id={"expert": to},
                    device_id_type=MESH,
                ).start()
        rx_same[j, 0] = tx[j, c * NZ + z]

    for q in range(NX):
        pltpu.make_async_remote_copy(
            src_ref=w_hbm.at[0, :, pl.ds(pl.multiple_of(q * 1024 + (1 - c) * HALF, HALF), HALF)],
            dst_ref=wbuf.at[1, q],
            send_sem=wr_sem.at[0],
            recv_sem=wr_sem.at[1],
            device_id={"dp": partner},
            device_id_type=MESH,
        ).start()

    cp_eo.wait()
    parts = [jnp.zeros((128, 128), F32) for _ in range(2)]
    for f in range(8):
        cols = slice(f * 128, (f + 1) * 128)
        grad = g[:, cols].astype(F32)
        both = eo[:, :, cols].astype(F32)
        for k in range(2):
            parts[k] = parts[k] + grad * both[:, k, :]
    score = [jnp.sum(parts[k].T, axis=0, keepdims=True) for k in range(2)]
    sub = lax.broadcasted_iota(jnp.int32, (8, 128), 0)
    sc_tx[...] = jnp.where(sub == 0, score[0], jnp.where(sub == 1, score[1], 0.0))
    for k in range(1, NX):
        pltpu.make_async_remote_copy(
            src_ref=sc_tx,
            dst_ref=sc_rx.at[k - 1],
            send_sem=sc_send.at[k - 1],
            recv_sem=sc_recv.at[k - 1],
            device_id={"tensor": (x + k) % NX},
            device_id_type=MESH,
        ).start()

    cp_gate.wait()
    cp_up.wait()
    for i in range(8):
        part = slice(i * 128, (i + 1) * 128)
        a = gate[part, :].astype(F32)
        b = up[part, :].astype(F32)
        sigma = 1.0 / (1.0 + jnp.exp(-a))
        fac_u[part, :] = a * sigma
        fac_g[part, :] = b * sigma * (1.0 + a * (1.0 - sigma))

    def place(ch, first, second):
        if ch == 0:
            return xs[first] * 4 + ys[second]
        return xs[second] * 4 + ys[first]

    def push(ch, j, first, second, along_first, way, part, slot):
        axis_x = along_first == (ch == 0)
        if axis_x:
            where = {"tensor": xs[way]}
        else:
            where = {"dp": ys[way] * 2 + c}
        ref = rows.at[ch, j, place(ch, first, second)]
        if part is not None:
            ref = ref.at[pl.ds(part * 32, 32)]
        pltpu.make_async_remote_copy(
            src_ref=ref,
            dst_ref=ref,
            send_sem=a_send.at[ch, j],
            recv_sem=a_recv.at[ch, j, slot],
            device_id=where,
            device_id_type=MESH,
        ).start()

    def arrived(ch, j, first, second, part, slot):
        ref = rows.at[ch, j, place(ch, first, second)]
        if part is not None:
            ref = ref.at[pl.ds(part * 32, 32)]
        pltpu.make_async_copy(ref, ref, a_recv.at[ch, j, slot]).wait()

    def spread(ch, j, first):
        push(ch, j, first, OWN, False, PLUS, None, 4 + 4 * first)
        push(ch, j, first, OWN, False, MINUS, None, 5 + 4 * first)

    def step_a(ch, j):
        push(ch, j, OWN, OWN, True, PLUS, None, 0)
        push(ch, j, OWN, OWN, True, MINUS, None, 1)
        spread(ch, j, OWN)

    def step_b(ch, j):
        arrived(ch, j, MINUS, OWN, None, 0)
        push(ch, j, MINUS, OWN, True, PLUS, 0, 2)
        spread(ch, j, MINUS)
        arrived(ch, j, PLUS, OWN, None, 1)
        push(ch, j, PLUS, OWN, True, MINUS, 1, 3)
        spread(ch, j, PLUS)

    def step_c(ch, j):
        arrived(ch, j, OPP, OWN, 0, 2)
        arrived(ch, j, OPP, OWN, 1, 3)
        spread(ch, j, OPP)

    def step_d(ch, j, first):
        arrived(ch, j, first, MINUS, None, 4 + 4 * first)
        push(ch, j, first, MINUS, False, PLUS, 0, 6 + 4 * first)
        arrived(ch, j, first, PLUS, None, 5 + 4 * first)
        push(ch, j, first, PLUS, False, MINUS, 1, 7 + 4 * first)

    def step_e(ch, j, first):
        arrived(ch, j, first, OPP, 0, 6 + 4 * first)
        arrived(ch, j, first, OPP, 1, 7 + 4 * first)

    out_row = lax.broadcasted_iota(jnp.int32, (256, 256), 0)
    in_row = lax.broadcasted_iota(jnp.int32, (256, 256), 1)
    src = (z + NZ - (out_row // 2) % 16) % NZ
    want = src * 16 + (out_row // 64) * 4 + ((out_row // 32) % 2) * 2 + out_row % 2
    perm = (in_row == want).astype(BF16)

    def unpack(j):
        pltpu.make_async_copy(rx_same.at[j, pl.ds(1, 15)], rx_same.at[j, pl.ds(1, 15)], z_recv.at[j, 0]).wait()
        pltpu.make_async_copy(rx_cross.at[j], rx_cross.at[j], z_recv.at[j, 1]).wait()
        for ch, ref in ((0, rx_same), (1, rx_cross)):
            out = jnp.dot(perm, ref[j].reshape(256, 128), preferred_element_type=F32).astype(BF16)
            for f in range(4):
                rows[ch, j, place(ch, OWN, OWN), :, f * 128 : (f + 1) * 128] = out[f * 64 : (f + 1) * 64]
            step_a(ch, j)

    def matmul(ch, j, rel):
        total = [None, None]
        for q in range(NX):
            block = rows[ch, j, q * 4 + ys[rel]]
            for side in (0, 1):
                term = lax.dot_general(
                    block, wbuf[side, q], (((1,), (1,)), ((), ())), preferred_element_type=F32
                )
                total[side] = term if total[side] is None else total[side] + term
        p_tx[ch, j, rel] = total[1]
        pltpu.make_async_remote_copy(
            src_ref=p_tx.at[ch, j, rel],
            dst_ref=p_rx.at[1 - ch, j, rel],
            send_sem=p_send.at[ch, j, rel],
            recv_sem=p_recv.at[1 - ch, j, rel],
            device_id={"dp": partner},
            device_id_type=MESH,
        ).start()
        p_own[ch, j, rel] = total[0]

    def finish(ch, j, rel):
        pltpu.make_async_copy(p_rx.at[ch, j, rel], p_rx.at[ch, j, rel], p_recv.at[ch, j, rel]).wait()
        hidden = p_own[ch, j, rel] + p_rx[ch, j, rel]
        core = c if ch == 0 else 1 - c
        at = pl.ds(pl.multiple_of((ys[rel] * 2 + core) * 128 + j * ROWS, ROWS), ROWS)
        out_u[at, :] = (hidden * fac_u[at, :]).astype(BF16)
        out_g[at, :] = (hidden * fac_g[at, :]).astype(BF16)
        pltpu.make_async_copy(out_u.at[at], ug_hbm.at[0, at], o_sem.at[0]).start()
        pltpu.make_async_copy(out_g.at[at], gg_hbm.at[0, at], o_sem.at[1]).start()

    def router_a():
        for k in range(1, NX):
            pltpu.make_async_copy(sc_rx.at[k - 1], sc_rx.at[k - 1], sc_recv.at[k - 1]).wait()
        total = sc_tx[...] + sc_rx[0] + sc_rx[1] + sc_rx[2]
        diff = total[0:1, :] * keep[0] - total[1:2, :] * keep[1]
        coef = wts[0] * wts[1] * diff
        logit_grad = coef * (hot[0] - hot[1])
        high = logit_grad.astype(BF16)
        rest = logit_grad - high.astype(F32)
        mid = rest.astype(BF16)
        low = (rest - mid.astype(F32)).astype(BF16)
        cp_tok.wait()
        terms = jnp.dot(
            jnp.concatenate([high, mid, low], axis=0), tok[...], preferred_element_type=F32
        )
        term = terms[0:16] + terms[16:32] + terms[32:48]
        for p in range(16):
            rt[p] = term[(p // 8) * 8 : (p // 8) * 8 + 8, (p % 8) * 128 : (p % 8) * 128 + 128]
        for k in range(1, NZ):
            to = (z + k) % NZ
            pltpu.make_async_remote_copy(
                src_ref=rt.at[to],
                dst_ref=r1.at[k - 1],
                send_sem=r_send.at[0],
                recv_sem=r_recv.at[0],
                device_id={"expert": to},
                device_id_type=MESH,
            ).start()

    def router_b():
        pltpu.make_async_copy(r1, r1, r_recv.at[0]).wait()
        total = rt[z]
        for k in range(NZ - 1):
            total = total + r1[k]
        r2[dp] = total
        for k in range(1, 2 * NY):
            pltpu.make_async_remote_copy(
                src_ref=r2.at[dp],
                dst_ref=r2.at[dp],
                send_sem=r_send.at[1],
                recv_sem=r_recv.at[1],
                device_id={"dp": (dp + k) % (2 * NY)},
                device_id_type=MESH,
            ).start()

    def router_c():
        pltpu.make_async_copy(r2.at[pl.ds(0, 7)], r2.at[pl.ds(0, 7)], r_recv.at[1]).wait()
        total = r2[0]
        for k in range(1, 2 * NY):
            total = total + r2[k]
        r3[z] = total
        for k in range(1, NZ):
            pltpu.make_async_remote_copy(
                src_ref=r3.at[z],
                dst_ref=r3.at[z],
                send_sem=r_send.at[2],
                recv_sem=r_recv.at[2],
                device_id={"expert": (z + k) % NZ},
                device_id_type=MESH,
            ).start()

    def router_d():
        pltpu.make_async_copy(r3.at[pl.ds(0, 15)], r3.at[pl.ds(0, 15)], r_recv.at[2]).wait()
        for p in range(16):
            rg_ref[(p // 8) * 8 : (p // 8) * 8 + 8, (p % 8) * 128 : (p % 8) * 128 + 128] = r3[p]

    unpack(0)
    router_a()
    step_b(0, 0)
    step_b(1, 0)
    unpack(1)
    step_c(0, 0)
    step_c(1, 0)
    step_d(0, 0, OWN)
    step_d(1, 0, OWN)
    step_b(0, 1)
    step_b(1, 1)
    router_b()
    pltpu.make_async_copy(wbuf.at[0], wbuf.at[0], w_sem.at[0]).wait()
    pltpu.make_async_copy(wbuf.at[1], wbuf.at[1], wr_sem.at[1]).wait()
    matmul(0, 0, OWN)
    step_d(0, 0, MINUS)
    step_d(1, 0, MINUS)
    step_c(0, 1)
    step_c(1, 1)
    step_d(0, 0, PLUS)
    step_d(1, 0, PLUS)
    step_d(0, 0, OPP)
    step_d(1, 0, OPP)
    step_e(1, 0, OWN)
    matmul(1, 0, OWN)
    finish(0, 0, OWN)
    matmul(0, 0, MINUS)
    step_d(0, 1, OWN)
    step_d(1, 1, OWN)
    finish(1, 0, OWN)
    matmul(0, 0, PLUS)
    router_c()
    matmul(0, 1, OWN)
    step_d(0, 1, MINUS)
    step_d(1, 1, MINUS)
    for first in (MINUS, PLUS):
        step_e(1, 0, first)
        matmul(1, 0, first)
        finish(0, 0, first)
    step_d(0, 1, PLUS)
    step_d(1, 1, PLUS)
    for first in range(4):
        step_e(0, 0, first)
    step_e(1, 0, OPP)
    matmul(0, 0, OPP)
    matmul(1, 0, OPP)
    step_d(0, 1, OPP)
    step_d(1, 1, OPP)
    finish(1, 0, MINUS)
    finish(1, 0, PLUS)
    step_e(1, 1, OWN)
    matmul(1, 1, OWN)
    matmul(0, 1, MINUS)
    matmul(0, 1, PLUS)
    finish(0, 0, OPP)
    finish(1, 0, OPP)
    finish(0, 1, OWN)
    router_d()
    for first in (MINUS, PLUS):
        step_e(1, 1, first)
        matmul(1, 1, first)
        finish(0, 1, first)
    finish(1, 1, OWN)
    finish(1, 1, MINUS)
    for first in range(4):
        step_e(0, 1, first)
    matmul(0, 1, OPP)
    step_e(1, 1, OPP)
    matmul(1, 1, OPP)
    finish(1, 1, PLUS)

    for j in range(NJ):
        pltpu.make_async_copy(tx.at[j, pl.ds(0, 31)], tx.at[j, pl.ds(0, 31)], z_send.at[j]).wait()
        for ch in range(2):
            sent = rows.at[ch, j, pl.ds(0, 15)]
            pltpu.make_async_copy(sent, sent, a_send.at[ch, j]).wait()
            for rel in range(NY):
                sent = p_tx.at[ch, j, rel]
                pltpu.make_async_copy(sent, sent, p_send.at[ch, j, rel]).wait()
    for k in range(NX - 1):
        pltpu.make_async_copy(sc_tx, sc_tx, sc_send.at[k]).wait()
    pltpu.make_async_copy(wbuf.at[1], wbuf.at[1], wr_sem.at[0]).wait()
    pltpu.make_async_copy(r1, r1, r_send.at[0]).wait()
    pltpu.make_async_copy(r2.at[pl.ds(0, 7)], r2.at[pl.ds(0, 7)], r_send.at[1]).wait()
    pltpu.make_async_copy(r1, r1, r_send.at[2]).wait()
    finish(0, 1, OPP)
    finish(1, 1, OPP)
    pltpu.make_async_copy(out_u, ug_hbm.at[0], o_sem.at[0]).wait()
    pltpu.make_async_copy(out_g, gg_hbm.at[0], o_sem.at[1]).wait()


def body(
    grad_out,
    tokens_in,
    router_logits,
    expert_ids,
    slot_index,
    kept,
    expert_out,
    gate_pre,
    up_pre,
    down_weight,
):
    anywhere = pl.BlockSpec(memory_space=pl.ANY)
    vmem = pl.BlockSpec(memory_space=pltpu.VMEM)
    dma = pltpu.SemaphoreType.DMA
    slots = gate_pre.shape[1]
    return pl.pallas_call(
        kernel,
        out_shape=(
            jax.ShapeDtypeStruct(gate_pre.shape, BF16),
            jax.ShapeDtypeStruct(gate_pre.shape, BF16),
            jax.ShapeDtypeStruct((16, 1024), F32),
        ),
        in_specs=[anywhere] * 6 + [vmem] * 4,
        out_specs=(anywhere, anywhere, vmem),
        scratch_shapes=[
            pltpu.VMEM((128, 1024), BF16),
            pltpu.VMEM((128, 1024), BF16),
            pltpu.VMEM((128, 2, 1024), BF16),
            pltpu.VMEM((slots, HID), BF16),
            pltpu.VMEM((slots, HID), BF16),
            pltpu.VMEM((2, NX, HID, HALF), BF16),
            pltpu.VMEM((slots, HID), F32),
            pltpu.VMEM((slots, HID), F32),
            pltpu.VMEM((slots, HID), BF16),
            pltpu.VMEM((slots, HID), BF16),
            pltpu.VMEM((NJ, 2 * NZ, 16, 128), BF16),
            pltpu.VMEM((NJ, NZ, 16, 128), BF16),
            pltpu.VMEM((NJ, NZ, 16, 128), BF16),
            pltpu.VMEM((2, NJ, NX * NY, ROWS, HALF), BF16),
            pltpu.VMEM((2, NJ, NY, ROWS, HID), F32),
            pltpu.VMEM((2, NJ, NY, ROWS, HID), F32),
            pltpu.VMEM((2, NJ, NY, ROWS, HID), F32),
            pltpu.VMEM((8, 128), F32),
            pltpu.VMEM((NX - 1, 8, 128), F32),
            pltpu.VMEM((NZ, 8, 128), F32),
            pltpu.VMEM((NZ - 1, 8, 128), F32),
            pltpu.VMEM((2 * NY, 8, 128), F32),
            pltpu.VMEM((NZ, 8, 128), F32),
            dma((5,)),
            dma((1,)),
            dma((2,)),
            dma((NJ,)),
            dma((NJ, 2)),
            dma((2, NJ)),
            dma((2, NJ, 20)),
            dma((2, NJ, NY)),
            dma((2, NJ, NY)),
            dma((NX - 1,)),
            dma((NX - 1,)),
            dma((3,)),
            dma((3,)),
            dma((2,)),
        ],
        compiler_params=pltpu.CompilerParams(
            collective_id=0, has_side_effects=True, vmem_limit_bytes=48 * 1024 * 1024
        ),
    )(
        grad_out,
        tokens_in,
        expert_out,
        gate_pre,
        up_pre,
        down_weight,
        router_logits.T,
        expert_ids.T,
        slot_index.T,
        kept.T,
    )


def solution(mesh):
    in_specs = (
        P(("dp", "expert"), "tensor"),
        P(("dp", "expert"), "tensor"),
        P(("dp", "expert"), None),
        P(("dp", "expert"), None),
        P(("dp", "expert"), None),
        P(("dp", "expert"), None),
        P(("dp", "expert"), None, "tensor"),
        P("expert", None, ("dp", "tensor")),
        P("expert", None, ("dp", "tensor")),
        P("expert", ("dp", "tensor"), None),
    )
    out_specs = (
        P("expert", None, ("dp", "tensor")),
        P("expert", None, ("dp", "tensor")),
        P(None, "tensor"),
    )
    return jax.shard_map(body, mesh=mesh, in_specs=in_specs, out_specs=out_specs, check_vma=False)
```

time: 411 us -> 80.2 us (0.20)
  waiting for transfers between devices: 330 us -> 0 us
  Pallas kernels: 0 us -> 69.2 us
  blocking collectives: 33.9 us -> 0 us
  between operations: 15.6 us -> 0.75 us
  matrix products: 10.9 us -> 0 us
  other arithmetic: 6.2 us -> 0 us
  local copies, waits for them, and re-layouts: 14.7 us -> 9.92 us
    psum x1 -> x0, waiting for transfers between devices: 239 us -> none  [body(): router_grad = lax.psum(router_term, ('dp', 'expert'))]
    all_gather x2 -> x0, waiting for transfers between devices: 89.6 us -> none  [the longest x1 67.7 us: body(): lax.all_gather(received, ('dp', 'tensor'), axis=0, tiled=True)]
    pallas_call x0 -> x1, Pallas kernels: none -> 69.2 us  [body(): pl.pallas_call(kernel, out_shape=(jax.ShapeDtypeStruct(gate_pre.shape, BF...]
    all_to_all x1 -> x0, blocking collectives: 24.6 us -> none  [body(): lax.all_to_all(outgoing, 'expert', split_axis=0, concat_axis=0, tiled=True)]
    mul x4 -> x0, local copies, waits for them, and re-layouts: 11.6 us -> none  [the longest x3 11.5 us: body(): (weights * keep_float)[:, :, None]]
    dot_general x3 -> x0, matrix products: 10.9 us -> none  [the longest x1 7.32 us: body(): lax.dot_general(lax.all_gather(received, ('dp', 'tensor'), axis=0, tiled=...]
    psum x1 -> x0, blocking collectives: 9.29 us -> none  [body(): scores = lax.psum(partial_scores, 'tensor') * keep_float]
    unnamed x9 -> x21, local copies, waits for them, and re-layouts: 1.49 us -> 6.95 us
  transfers between devices with their start and end apart: 3 -> 0, of which waited for: 3 -> 0; matrix products, arithmetic and copies ran while one was open for 4% -> 0% of each run, Pallas kernels for 0% -> 0%
where the time goes in v1:
time: 80.2 us; the launch traced here: 79.9 us
  Pallas kernels  69.2 us (86%)
  local copies, waits for them, and re-layouts  9.92 us (12%)
    pallas_call x1, Pallas kernels, body(): pl.pallas_call(kernel, out_shape=(jax.ShapeDtypeStruct(gate_pre.shape, BF...  69.2 us
    unnamed x21, local copies, waits for them, and re-layouts  6.95 us
    pallas_call x2, local copies, waits for them, and re-layouts, body(): pl.pallas_call(kernel, out_shape=(jax.ShapeDtypeStruct(gate_pre.shape, BF...  2.97 us

profile of v1, /device:TPU:1, one launch (start us, length us, event | category | flops | bytes accessed | tf_op | source)
XLA Modules:
  0.0 79.9 jit_solution(3585949236512800273)
XLA Ops:
  0.6 0.0 copy-start
  0.6 0.0 copy-start.8
  0.7 0.0 copy-start.7
  0.7 0.0 copy-start.6
  0.7 0.0 copy-start.5
  0.7 1.3 %copy.13.gate_hbm = bf16[1,1024,224]{2,1,0:T(8,128)(2,1)S(1)} copy(bf16[1,1024,224]{1,2,0:T(8,128)(2,1)} %param.17) | data formatting | bytes 917504 | tf_op args[7]
  2.0 1.2 %copy.14.up_hbm = bf16[1,1024,224]{2,1,0:T(8,128)(2,1)S(1)} copy(bf16[1,1024,224]{1,2,0:T(8,128)(2,1)} %param.18) | data formatting | bytes 917504 | tf_op args[8]
  3.3 0.0 copy-done
  3.3 0.0 copy-done.8
  3.3 0.0 copy-done.7
  3.3 0.0 copy-done.6
  3.3 0.0 copy-done.5
  3.3 0.0 copy-start.1
  3.3 1.0 %copy-done.1 = bf16[128,2,1024]{2,1,0:T(2,128)(2,1)S(1)} copy-done((bf16[128,2,1024]{2,1,0:T(2,128)(2,1)S(1)}, bf16[128,2,1024]{2,1,0:T(2,128)(2,1)}, u32[]{:S(2)}) %copy-start.1) | copy-done | bytes 524312
  4.4 0.0 copy-start.3
  4.4 0.9 %copy-done.3 = bf16[128,1024]{1,0:T(8,128)(2,1)S(1)} copy-done((bf16[128,1024]{1,0:T(8,128)(2,1)S(1)}, bf16[128,1024]{1,0:T(8,128)(2,1)}, u32[]{:S(2)}) %copy-start.3) | copy-done | bytes 262168
  5.3 0.0 copy-start.4
  5.3 0.9 %copy-done.4 = bf16[128,1024]{1,0:T(8,128)(2,1)S(1)} copy-done((bf16[128,1024]{1,0:T(8,128)(2,1)S(1)}, bf16[128,1024]{1,0:T(8,128)(2,1)}, u32[]{:S(2)}) %copy-start.4) | copy-done | bytes 262168
  6.3 69.2 %shard_map.121 = (bf16[1,1024,224]{2,1,0:T(8,128)(2,1)S(1)}, bf16[1,1024,224]{2,1,0:T(8,128)(2,1)S(1)}, f32[16,1024]{1,0:T(8,128)S(1)}) custom-call(bf16[128,1024]{1,0:T(8,128)(2,1)S(1)} %copy-done.3, bf16[128,1024]{1,0:T(8,128)(2,1)S(1)} %copy-done.4, bf16[128,2,1024]{2,1,0:T(2,128)(2,1)S(1)} %copy-done.1, bf16[1,1024,224]{2,1,0:T(8,128)(2,1)S(1)} %copy.13.gate_hbm, ...), custom_call_target="tpu_custom_call" | custom-call | tf_op jit(solution)/shard_map/pallas_call | solution.py:461
  75.5 0.0 copy-start.2
  75.5 0.8 copy-done.2
  76.3 2.0 %copy.15 = bf16[1,1024,224]{1,2,0:T(8,128)(2,1)} copy(bf16[1,1024,224]{2,1,0:T(8,128)(2,1)} %copy-done.2) | data formatting | bytes 917504 | tf_op jit(solution)/shard_map/pallas_call | solution.py:461
  78.3 1.0 %copy.16 = bf16[1,1024,224]{1,2,0:T(8,128)(2,1)} copy(bf16[1,1024,224]{2,1,0:T(8,128)(2,1)S(1)} %get-tuple-element.4) | data formatting | bytes 917504 | tf_op jit(solution)/shard_map/pallas_call | solution.py:461
  79.3 0.6 copy.18
Async XLA Ops:
  0.6 2.6 %copy-start = (bf16[1,224,4096]{2,1,0:T(8,128)(2,1)S(1)}, bf16[1,224,4096]{2,1,0:T(8,128)(2,1)}, u32[]{:S(2)}) copy-start(bf16[1,224,4096]{2,1,0:T(8,128)(2,1)} %w_hbm.1) | copy-start | bytes 5505028
  0.6 2.6 %copy-start.8 = (s32[128,2]{0,1:T(2,128)S(1)}, s32[128,2]{0,1:T(2,128)}, u32[]{:S(2)}) copy-start(s32[128,2]{0,1:T(2,128)} %param.15) | copy-start | bytes 3076
  0.7 2.6 %copy-start.7 = (s32[128,2]{0,1:T(2,128)S(1)}, s32[128,2]{0,1:T(2,128)}, u32[]{:S(2)}) copy-start(s32[128,2]{0,1:T(2,128)} %param.14) | copy-start | bytes 3076
  0.7 2.6 %copy-start.6 = (s32[128,2]{0,1:T(2,128)S(1)}, s32[128,2]{0,1:T(2,128)}, u32[]{:S(2)}) copy-start(s32[128,2]{0,1:T(2,128)} %param.13) | copy-start | bytes 3076
  0.7 2.6 %copy-start.5 = (f32[128,16]{0,1:T(8,128)S(1)}, f32[128,16]{0,1:T(8,128)}, u32[]{:S(2)}) copy-start(f32[128,16]{0,1:T(8,128)} %param.12) | copy-start | bytes 24580
  3.3 1.0 %copy-start.1 = (bf16[128,2,1024]{2,1,0:T(2,128)(2,1)S(1)}, bf16[128,2,1024]{2,1,0:T(2,128)(2,1)}, u32[]{:S(2)}) copy-start(bf16[128,2,1024]{2,1,0:T(2,128)(2,1)} %eo_hbm.1) | copy-start | bytes 1572868
  4.4 0.9 %copy-start.3 = (bf16[128,1024]{1,0:T(8,128)(2,1)S(1)}, bf16[128,1024]{1,0:T(8,128)(2,1)}, u32[]{:S(2)}) copy-start(bf16[128,1024]{1,0:T(8,128)(2,1)} %g_hbm.1) | copy-start | bytes 786436
  5.3 0.9 %copy-start.4 = (bf16[128,1024]{1,0:T(8,128)(2,1)S(1)}, bf16[128,1024]{1,0:T(8,128)(2,1)}, u32[]{:S(2)}) copy-start(bf16[128,1024]{1,0:T(8,128)(2,1)} %tok_hbm.1) | copy-start | bytes 786436
  75.5 0.8 copy-start.2

commit v2 on v1

v2 whole, which is shorter than its diff:
```python
import functools

import jax
import jax.numpy as jnp
from jax import lax
from jax.experimental import pallas as pl
from jax.experimental.pallas import tpu as pltpu
from jax.sharding import PartitionSpec as P

MESH = pl.DeviceIdType.MESH
F32 = jnp.float32
BF16 = jnp.bfloat16

NZ = 16
NX = 4
NY = 4
NJ = 2
HID = 224
HALF = 512
ROWS = 128
PART = HALF // NJ

DISPATCH = True
GATHER = True
MATMUL = True
ROUTER = True

OWN, MINUS, PLUS, OPP = 0, 1, 2, 3


def kernel(
    g_hbm, tok_hbm, eo_hbm, gate_hbm, up_hbm, w_hbm, logits_hbm, ids_hbm, slot_hbm, kept_hbm,
    gg_ref, ug_ref, rg_ref,
    g, tok, eo, gate, up, logits_ref, ids_ref, slot_ref, kept_ref, wbuf, fac_u, fac_g,
    tx, rx_same, rx_cross, rows, p_own, p_tx, p_rx,
    sc_tx, sc_rx, rt, r1, r2, r3,
    in_sem, w_sem, wr_sem, z_send, z_recv, a_send, a_recv, p_send, p_recv,
    sc_send, sc_recv, r_send, r_recv,
):
    dp = lax.axis_index("dp")
    z = lax.axis_index("expert")
    x = lax.axis_index("tensor")
    y = dp // 2
    c = dp % 2
    partner = dp + 1 - 2 * c
    xs = [x, (x + 3) % 4, (x + 1) % 4, (x + 2) % 4]
    ys = [y, (y + 3) % 4, (y + 1) % 4, (y + 2) % 4]

    def fetch(i, src, dst):
        copy = pltpu.make_async_copy(src, dst, in_sem.at[i])
        copy.start()
        return copy

    routes = [
        fetch(5, logits_hbm, logits_ref),
        fetch(6, ids_hbm, ids_ref),
        fetch(7, slot_hbm, slot_ref),
        fetch(8, kept_hbm, kept_ref),
    ]
    cp_g = fetch(0, g_hbm, g)

    barrier = pltpu.get_barrier_semaphore()

    def greet(**where):
        pl.semaphore_signal(barrier, inc=1, device_id=where, device_id_type=MESH)

    far_first = [NZ // 2]
    for k in range(NZ // 2 - 1, 0, -1):
        far_first += [k, NZ - k]
    for k in far_first:
        greet(expert=(z + k) % NZ)
        greet(expert=(z + k) % NZ, dp=partner)
    for k in range(1, NX):
        greet(tensor=(x + k) % NX)
    for k in range(1, 2 * NY):
        greet(dp=(dp + k) % (2 * NY))

    cp_eo = fetch(1, eo_hbm, eo)
    cp_tok = fetch(2, tok_hbm, tok)
    cp_gate = fetch(3, gate_hbm.at[0], gate)
    cp_up = fetch(4, up_hbm.at[0], up)
    for q in range(NX):
        pltpu.make_async_copy(
            w_hbm.at[0, :, pl.ds(pl.multiple_of(q * 1024 + c * HALF, HALF), HALF)],
            wbuf.at[0, q],
            w_sem.at[0],
        ).start()

    for copy in routes:
        copy.wait()
    ids = ids_ref[...]
    slots = slot_ref[...]
    kept = kept_ref[...]
    logits = logits_ref[...]
    expert_row = lax.broadcasted_iota(jnp.int32, (16, 128), 0)
    hot = [(expert_row == ids[k : k + 1, :]).astype(F32) for k in range(2)]
    chosen = [jnp.sum(hot[k] * logits, axis=0, keepdims=True) for k in range(2)]
    w0 = 1.0 / (1.0 + jnp.exp(chosen[1] - chosen[0]))
    wts = [w0, 1.0 - w0]
    keep = [kept[k : k + 1, :].astype(F32) for k in range(2)]

    row = lax.broadcasted_iota(jnp.int32, (256, 128), 0)
    row_key = (row // 16) * 8 + row % 8
    row_blk = (row // 8) % 2
    one = jnp.zeros((256, 128), F32)
    val = jnp.zeros((256, 128), F32)
    for k in range(2):
        key = jnp.where(kept[k : k + 1, :] == 1, ids[k : k + 1, :] * 8 + slots[k : k + 1, :], -1)
        hit = (row_key == key).astype(F32)
        one = one + hit
        val = val + hit * wts[k]
    scale = jnp.sum(val, axis=1, keepdims=True)
    wide = jnp.concatenate(
        [jnp.where(row_blk == f, one, 0.0).astype(BF16) for f in range(2)], axis=1
    )
    cp_g.wait()
    for j in range(NJ):
        for h in range(2):
            at = h * HALF + j * PART
            tall = jnp.concatenate([g[:, at : at + 128], g[:, at + 128 : at + 256]], axis=0)
            picked = jnp.dot(wide, tall, preferred_element_type=F32)
            tx[j, h * NZ : (h + 1) * NZ] = (picked * scale).astype(BF16).reshape(NZ, 16, 128)

    pl.semaphore_wait(barrier, 2 * (NZ - 1) + (NX - 1) + (2 * NY - 1))

    for j in range(NJ if DISPATCH else 0):
        rx_same[j, 0] = tx[j, c * NZ + z]
        for k in far_first:
            to = (z + k) % NZ
            pltpu.make_async_remote_copy(
                src_ref=tx.at[j, c * NZ + to],
                dst_ref=rx_same.at[j, k],
                send_sem=z_send.at[j],
                recv_sem=z_recv.at[j, 0],
                device_id={"expert": to},
                device_id_type=MESH,
            ).start()
        for k in far_first + [0]:
            to = (z + k) % NZ
            pltpu.make_async_remote_copy(
                src_ref=tx.at[j, (1 - c) * NZ + to],
                dst_ref=rx_cross.at[j, k],
                send_sem=z_send.at[j],
                recv_sem=z_recv.at[j, 1],
                device_id={"expert": to, "dp": partner},
                device_id_type=MESH,
            ).start()

    for q in range(NX):
        pltpu.make_async_remote_copy(
            src_ref=w_hbm.at[0, :, pl.ds(pl.multiple_of(q * 1024 + (1 - c) * HALF, HALF), HALF)],
            dst_ref=wbuf.at[1, q],
            send_sem=wr_sem.at[0],
            recv_sem=wr_sem.at[1],
            device_id={"dp": partner},
            device_id_type=MESH,
        ).start()

    cp_eo.wait()
    parts = [jnp.zeros((128, 128), F32) for _ in range(2)]
    for f in range(8):
        cols = slice(f * 128, (f + 1) * 128)
        grad = g[:, cols].astype(F32)
        both = eo[:, :, cols].astype(F32)
        for k in range(2):
            parts[k] = parts[k] + grad * both[:, k, :]
    score = [jnp.sum(parts[k].T, axis=0, keepdims=True) for k in range(2)]
    sub = lax.broadcasted_iota(jnp.int32, (8, 128), 0)
    sc_tx[...] = jnp.where(sub == 0, score[0], jnp.where(sub == 1, score[1], 0.0))
    for k in range(1, NX if ROUTER else 1):
        pltpu.make_async_remote_copy(
            src_ref=sc_tx,
            dst_ref=sc_rx.at[k - 1],
            send_sem=sc_send.at[k - 1],
            recv_sem=sc_recv.at[k - 1],
            device_id={"tensor": (x + k) % NX},
            device_id_type=MESH,
        ).start()

    cp_gate.wait()
    cp_up.wait()
    for i in range(8):
        part = slice(i * 128, (i + 1) * 128)
        a = gate[:, part].astype(F32)
        b = up[:, part].astype(F32)
        sigma = 1.0 / (1.0 + jnp.exp(-a))
        fac_u[:, part] = a * sigma
        fac_g[:, part] = b * sigma * (1.0 + a * (1.0 - sigma))

    def place(ch, first, second):
        if ch == 0:
            return xs[first] * 4 + ys[second]
        return xs[second] * 4 + ys[first]

    def side_of(ch):
        return c if ch == 0 else 1 - c

    def push(ch, j, first, second, along_first, way, part, slot):
        if not GATHER:
            return
        axis_x = along_first == (ch == 0)
        if axis_x:
            where = {"tensor": xs[way]}
        else:
            where = {"dp": ys[way] * 2 + c}
        ref = rows.at[j, place(ch, first, second), side_of(ch)]
        if part is not None:
            ref = ref.at[pl.ds(part * 64, 64)]
        pltpu.make_async_remote_copy(
            src_ref=ref,
            dst_ref=ref,
            send_sem=a_send.at[j],
            recv_sem=a_recv.at[ch, j, slot],
            device_id=where,
            device_id_type=MESH,
        ).start()

    def arrived(ch, j, first, second, part, slot):
        if not GATHER:
            return
        ref = rows.at[j, place(ch, first, second), side_of(ch)]
        if part is not None:
            ref = ref.at[pl.ds(part * 64, 64)]
        pltpu.make_async_copy(ref, ref, a_recv.at[ch, j, slot]).wait()

    def spread(ch, j, first):
        push(ch, j, first, OWN, False, PLUS, None, 4 + 4 * first)
        push(ch, j, first, OWN, False, MINUS, None, 5 + 4 * first)

    def step_a(ch, j):
        push(ch, j, OWN, OWN, True, PLUS, None, 0)
        push(ch, j, OWN, OWN, True, MINUS, None, 1)
        spread(ch, j, OWN)

    def step_b(ch, j):
        arrived(ch, j, MINUS, OWN, None, 0)
        push(ch, j, MINUS, OWN, True, PLUS, 0, 2)
        spread(ch, j, MINUS)
        arrived(ch, j, PLUS, OWN, None, 1)
        push(ch, j, PLUS, OWN, True, MINUS, 1, 3)
        spread(ch, j, PLUS)

    def step_c(ch, j):
        arrived(ch, j, OPP, OWN, 0, 2)
        arrived(ch, j, OPP, OWN, 1, 3)
        spread(ch, j, OPP)

    def step_d(ch, j, first):
        arrived(ch, j, first, MINUS, None, 4 + 4 * first)
        push(ch, j, first, MINUS, False, PLUS, 0, 6 + 4 * first)
        arrived(ch, j, first, PLUS, None, 5 + 4 * first)
        push(ch, j, first, PLUS, False, MINUS, 1, 7 + 4 * first)

    def step_e(ch, j, first):
        arrived(ch, j, first, OPP, 0, 6 + 4 * first)
        arrived(ch, j, first, OPP, 1, 7 + 4 * first)

    out_row = lax.broadcasted_iota(jnp.int32, (256, 256), 0)
    in_row = lax.broadcasted_iota(jnp.int32, (256, 256), 1)
    src = (z + NZ - (out_row // 2) % 16) % NZ
    want = src * 16 + (out_row // 128) * 8 + ((out_row // 32) % 4) * 2 + out_row % 2
    perm = (in_row == want).astype(BF16)

    def unpack(ch, j):
        if DISPATCH:
            got = (rx_same.at[j, pl.ds(1, 15)], rx_cross.at[j])[ch]
            pltpu.make_async_copy(got, got, z_recv.at[j, ch]).wait()
        packets = (rx_same, rx_cross)[ch][j].reshape(256, 128)
        out = jnp.dot(perm, packets, preferred_element_type=F32).astype(BF16)
        for f in range(2):
            rows[j, place(ch, OWN, OWN), side_of(ch), :, f * 128 : (f + 1) * 128] = out[f * 128 : (f + 1) * 128]
        step_a(ch, j)

    def matmul(j, rel):
        if not MATMUL:
            return
        total = [None, None]
        for q in range(NX):
            block = rows[j, q * 4 + ys[rel]].reshape(2 * ROWS, PART)
            for side in (0, 1):
                term = lax.dot_general(
                    wbuf[side, q, :, j * PART : (j + 1) * PART],
                    block,
                    (((1,), (1,)), ((), ())),
                    preferred_element_type=F32,
                )
                total[side] = term if total[side] is None else total[side] + term
        if j == 0:
            p_own[rel] = total[0]
            p_tx[rel] = total[1]
            return
        p_tx[rel] = p_tx[rel] + total[1]
        pltpu.make_async_remote_copy(
            src_ref=p_tx.at[rel],
            dst_ref=p_rx.at[rel],
            send_sem=p_send.at[rel],
            recv_sem=p_recv.at[rel],
            device_id={"dp": partner},
            device_id_type=MESH,
        ).start()
        p_own[rel] = p_own[rel] + total[0]

    def finish(rel):
        if not MATMUL:
            return
        pltpu.make_async_copy(p_rx.at[rel], p_rx.at[rel], p_recv.at[rel]).wait()
        hidden = p_own[rel] + p_rx[rel]
        at = pl.ds(pl.multiple_of(ys[rel] * 256, 256), 256)
        ug_ref[0, :, at] = (hidden * fac_u[:, at]).astype(BF16)
        gg_ref[0, :, at] = (hidden * fac_g[:, at]).astype(BF16)

    def router_a():
        if not ROUTER:
            return
        for k in range(1, NX):
            pltpu.make_async_copy(sc_rx.at[k - 1], sc_rx.at[k - 1], sc_recv.at[k - 1]).wait()
        total = sc_tx[...] + sc_rx[0] + sc_rx[1] + sc_rx[2]
        diff = total[0:1, :] * keep[0] - total[1:2, :] * keep[1]
        coef = wts[0] * wts[1] * diff
        logit_grad = coef * (hot[0] - hot[1])
        high = logit_grad.astype(BF16)
        rest = logit_grad - high.astype(F32)
        mid = rest.astype(BF16)
        low = (rest - mid.astype(F32)).astype(BF16)
        cp_tok.wait()
        terms = jnp.dot(
            jnp.concatenate([high, mid, low], axis=0), tok[...], preferred_element_type=F32
        )
        term = terms[0:16] + terms[16:32] + terms[32:48]
        for p in range(16):
            rt[p] = term[(p // 8) * 8 : (p // 8) * 8 + 8, (p % 8) * 128 : (p % 8) * 128 + 128]
        for k in range(1, NZ):
            to = (z + k) % NZ
            pltpu.make_async_remote_copy(
                src_ref=rt.at[to],
                dst_ref=r1.at[k - 1],
                send_sem=r_send.at[0],
                recv_sem=r_recv.at[0],
                device_id={"expert": to},
                device_id_type=MESH,
            ).start()

    def router_b():
        if not ROUTER:
            return
        pltpu.make_async_copy(r1, r1, r_recv.at[0]).wait()
        total = rt[z]
        for k in range(NZ - 1):
            total = total + r1[k]
        r2[dp] = total
        for k in range(1, 2 * NY):
            pltpu.make_async_remote_copy(
                src_ref=r2.at[dp],
                dst_ref=r2.at[dp],
                send_sem=r_send.at[1],
                recv_sem=r_recv.at[1],
                device_id={"dp": (dp + k) % (2 * NY)},
                device_id_type=MESH,
            ).start()

    def router_c():
        if not ROUTER:
            return
        pltpu.make_async_copy(r2.at[pl.ds(0, 7)], r2.at[pl.ds(0, 7)], r_recv.at[1]).wait()
        total = r2[0]
        for k in range(1, 2 * NY):
            total = total + r2[k]
        r3[z] = total
        for k in range(1, NZ):
            pltpu.make_async_remote_copy(
                src_ref=r3.at[z],
                dst_ref=r3.at[z],
                send_sem=r_send.at[2],
                recv_sem=r_recv.at[2],
                device_id={"expert": (z + k) % NZ},
                device_id_type=MESH,
            ).start()

    def router_d():
        if not ROUTER:
            return
        pltpu.make_async_copy(r3.at[pl.ds(0, 15)], r3.at[pl.ds(0, 15)], r_recv.at[2]).wait()
        for p in range(16):
            rg_ref[(p // 8) * 8 : (p // 8) * 8 + 8, (p % 8) * 128 : (p % 8) * 128 + 128] = r3[p]

    def unpacked(t):
        unpack(t % 2, t // 2)

    def near(t):
        step_b(t % 2, t // 2)

    def across(t):
        step_c(t % 2, t // 2)

    def onward(t, first):
        step_d(t % 2, t // 2, first)

    def last(t):
        for first in range(4):
            step_e(t % 2, t // 2, first)

    unpacked(0)
    router_a()
    unpacked(1)
    near(0)
    onward(0, OWN)
    unpacked(2)
    across(0)
    near(1)
    onward(1, OWN)
    unpacked(3)
    onward(0, MINUS)
    across(1)
    near(2)
    onward(2, OWN)
    onward(0, PLUS)
    router_b()
    near(3)
    onward(1, MINUS)
    onward(3, OWN)
    across(2)
    onward(0, OPP)
    across(3)
    onward(1, PLUS)
    onward(2, MINUS)
    onward(1, OPP)
    onward(3, MINUS)
    pltpu.make_async_copy(wbuf.at[0], wbuf.at[0], w_sem.at[0]).wait()
    pltpu.make_async_copy(wbuf.at[1], wbuf.at[1], wr_sem.at[1]).wait()
    step_e(1, 0, OWN)
    matmul(0, OWN)
    router_c()
    onward(2, PLUS)
    step_e(1, 0, MINUS)
    matmul(0, MINUS)
    onward(3, PLUS)
    step_e(1, 0, PLUS)
    matmul(0, PLUS)
    onward(2, OPP)
    step_e(1, 0, OPP)
    for first in range(4):
        step_e(0, 0, first)
    matmul(0, OPP)
    onward(3, OPP)
    step_e(1, 1, OWN)
    matmul(1, OWN)
    step_e(1, 1, MINUS)
    matmul(1, MINUS)
    step_e(1, 1, PLUS)
    matmul(1, PLUS)
    router_d()
    finish(OWN)
    for first in range(4):
        step_e(0, 1, first)
    step_e(1, 1, OPP)
    matmul(1, OPP)
    finish(MINUS)
    finish(PLUS)
    if not ROUTER:
        cp_tok.wait()

    for j in range(NJ):
        if DISPATCH:
            pltpu.make_async_copy(tx.at[j, pl.ds(0, 31)], tx.at[j, pl.ds(0, 31)], z_send.at[j]).wait()
        if GATHER:
            sent = rows.at[j, pl.ds(0, 15)]
            pltpu.make_async_copy(sent, sent, a_send.at[j]).wait()
    if ROUTER:
        for k in range(NX - 1):
            pltpu.make_async_copy(sc_tx, sc_tx, sc_send.at[k]).wait()
        pltpu.make_async_copy(r1, r1, r_send.at[0]).wait()
        pltpu.make_async_copy(r2.at[pl.ds(0, 7)], r2.at[pl.ds(0, 7)], r_send.at[1]).wait()
        pltpu.make_async_copy(r1, r1, r_send.at[2]).wait()
    pltpu.make_async_copy(wbuf.at[1], wbuf.at[1], wr_sem.at[0]).wait()
    finish(OPP)
    if MATMUL:
        for rel in range(NY):
            pltpu.make_async_copy(p_tx.at[rel], p_tx.at[rel], p_send.at[rel]).wait()


def body(
    grad_out,
    tokens_in,
    router_logits,
    expert_ids,
    slot_index,
    kept,
    expert_out,
    gate_pre,
    up_pre,
    down_weight,
):
    hbm = pl.BlockSpec(memory_space=pltpu.HBM)
    vmem = pl.BlockSpec(memory_space=pltpu.VMEM)
    dma = pltpu.SemaphoreType.DMA
    slots = gate_pre.shape[1]
    gate_grad, up_grad, router_grad = pl.pallas_call(
        kernel,
        out_shape=(
            jax.ShapeDtypeStruct((1, HID, slots), BF16),
            jax.ShapeDtypeStruct((1, HID, slots), BF16),
            jax.ShapeDtypeStruct((16, 1024), F32),
        ),
        in_specs=[hbm] * 10,
        out_specs=(vmem, vmem, vmem),
        scratch_shapes=[
            pltpu.VMEM((128, 1024), BF16),
            pltpu.VMEM((128, 1024), BF16),
            pltpu.VMEM((128, 2, 1024), BF16),
            pltpu.VMEM((HID, slots), BF16),
            pltpu.VMEM((HID, slots), BF16),
            pltpu.VMEM((16, 128), F32),
            pltpu.VMEM((2, 128), jnp.int32),
            pltpu.VMEM((2, 128), jnp.int32),
            pltpu.VMEM((2, 128), jnp.int32),
            pltpu.VMEM((2, NX, HID, HALF), BF16),
            pltpu.VMEM((HID, slots), F32),
            pltpu.VMEM((HID, slots), F32),
            pltpu.VMEM((NJ, 2 * NZ, 16, 128), BF16),
            pltpu.VMEM((NJ, NZ, 16, 128), BF16),
            pltpu.VMEM((NJ, NZ, 16, 128), BF16),
            pltpu.VMEM((NJ, NX * NY, 2, ROWS, PART), BF16),
            pltpu.VMEM((NY, HID, 2 * ROWS), F32),
            pltpu.VMEM((NY, HID, 2 * ROWS), F32),
            pltpu.VMEM((NY, HID, 2 * ROWS), F32),
            pltpu.VMEM((8, 128), F32),
            pltpu.VMEM((NX - 1, 8, 128), F32),
            pltpu.VMEM((NZ, 8, 128), F32),
            pltpu.VMEM((NZ - 1, 8, 128), F32),
            pltpu.VMEM((2 * NY, 8, 128), F32),
            pltpu.VMEM((NZ, 8, 128), F32),
            dma((9,)),
            dma((1,)),
            dma((2,)),
            dma((NJ,)),
            dma((NJ, 2)),
            dma((NJ,)),
            dma((2, NJ, 20)),
            dma((NY,)),
            dma((NY,)),
            dma((NX - 1,)),
            dma((NX - 1,)),
            dma((3,)),
            dma((3,)),
        ],
        compiler_params=pltpu.CompilerParams(
            collective_id=0, has_side_effects=True, vmem_limit_bytes=24 * 1024 * 1024
        ),
    )(
        *(
            pltpu.with_memory_space_constraint(arg, pltpu.HBM)
            for arg in (
                grad_out,
                tokens_in,
                expert_out,
                jnp.swapaxes(gate_pre, 1, 2),
                jnp.swapaxes(up_pre, 1, 2),
                down_weight,
                router_logits.T,
                expert_ids.T,
                slot_index.T,
                kept.T,
            )
        )
    )
    return jnp.swapaxes(gate_grad, 1, 2), jnp.swapaxes(up_grad, 1, 2), router_grad


def solution(mesh):
    in_specs = (
        P(("dp", "expert"), "tensor"),
        P(("dp", "expert"), "tensor"),
        P(("dp", "expert"), None),
        P(("dp", "expert"), None),
        P(("dp", "expert"), None),
        P(("dp", "expert"), None),
        P(("dp", "expert"), None, "tensor"),
        P("expert", None, ("dp", "tensor")),
        P("expert", None, ("dp", "tensor")),
        P("expert", ("dp", "tensor"), None),
    )
    out_specs = (
        P("expert", None, ("dp", "tensor")),
        P("expert", None, ("dp", "tensor")),
        P(None, "tensor"),
    )
    return jax.shard_map(body, mesh=mesh, in_specs=in_specs, out_specs=out_specs, check_vma=False)
```

time: 80.2 us -> 62 us (0.77)
  Pallas kernels: 69.2 us -> 59.1 us
  local copies, waits for them, and re-layouts: 9.92 us -> 2.17 us
    pallas_call x1, Pallas kernels: 69.2 us -> 59.1 us  [body(): pl.pallas_call(kernel, out_shape=(jax.ShapeDtypeStruct((1, HID, slots), B...]
    unnamed x21 -> x3, local copies, waits for them, and re-layouts: 6.95 us -> 2.17 us
    pallas_call x2 -> x0, local copies, waits for them, and re-layouts: 2.97 us -> none  [body(): pl.pallas_call(kernel, out_shape=(jax.ShapeDtypeStruct(gate_pre.shape, BF...]
where the time goes in v2:
time: 62 us; the launch traced here: 61.9 us
  Pallas kernels  59.1 us (95%)
  local copies, waits for them, and re-layouts  2.17 us (4%)
  between operations  0.64 us (1%)
    pallas_call x1, Pallas kernels, body(): pl.pallas_call(kernel, out_shape=(jax.ShapeDtypeStruct((1, HID, slots), B...  59.1 us
    unnamed x3, local copies, waits for them, and re-layouts  2.17 us

profile of v2, /device:TPU:1, one launch (start us, length us, event | category | flops | bytes accessed | tf_op | source)
XLA Modules:
  0.0 61.9 jit_solution(14213007832387117187)
XLA Ops:
  0.6 59.1 %shard_map.121 = (bf16[1,224,1024]{2,1,0:T(8,128)(2,1)S(1)}, bf16[1,224,1024]{2,1,0:T(8,128)(2,1)S(1)}, f32[16,1024]{1,0:T(8,128)S(1)}) custom-call(bf16[128,1024]{1,0:T(8,128)(2,1)} %g_hbm.1, bf16[128,1024]{1,0:T(8,128)(2,1)} %tok_hbm.1, bf16[128,2,1024]{2,1,0:T(2,128)(2,1)} %eo_hbm.1, bf16[1,224,1024]{2,1,0:T(8,128)(2,1)} %bitcast.10, ...), custom_call_target="tpu_custom_call" | custom-call | tf_op jit(solution)/shard_map/pallas_call | solution.py:497
  59.7 0.8 %copy.16 = bf16[1,1024,224]{1,2,0:T(8,128)(2,1)} copy(bf16[1,1024,224]{1,2,0:T(8,128)(2,1)S(1)} %bitcast.9) | data formatting | bytes 917504
  60.5 0.8 %copy.17 = bf16[1,1024,224]{1,2,0:T(8,128)(2,1)} copy(bf16[1,1024,224]{1,2,0:T(8,128)(2,1)S(1)} %bitcast.8) | data formatting | bytes 917504
  61.3 0.6 %copy.18 = f32[16,1024]{1,0:T(8,128)} copy(f32[16,1024]{1,0:T(8,128)S(1)} %get-tuple-element.14) | data formatting | bytes 131072

commit v3 on v2

--- a/solution.py
+++ b/solution.py
@@ -19,11 +19,6 @@
 HALF = 512
 ROWS = 128
 PART = HALF // NJ
-
-DISPATCH = True
-GATHER = True
-MATMUL = True
-ROUTER = True
 
 OWN, MINUS, PLUS, OPP = 0, 1, 2, 3
 
@@ -75,17 +70,6 @@
     for k in range(1, 2 * NY):
         greet(dp=(dp + k) % (2 * NY))
 
-    cp_eo = fetch(1, eo_hbm, eo)
-    cp_tok = fetch(2, tok_hbm, tok)
-    cp_gate = fetch(3, gate_hbm.at[0], gate)
-    cp_up = fetch(4, up_hbm.at[0], up)
-    for q in range(NX):
-        pltpu.make_async_copy(
-            w_hbm.at[0, :, pl.ds(pl.multiple_of(q * 1024 + c * HALF, HALF), HALF)],
-            wbuf.at[0, q],
-            w_sem.at[0],
-        ).start()
-
     for copy in routes:
         copy.wait()
     ids = ids_ref[...]
@@ -114,16 +98,20 @@
         [jnp.where(row_blk == f, one, 0.0).astype(BF16) for f in range(2)], axis=1
     )
     cp_g.wait()
-    for j in range(NJ):
+
+    def pack(j):
         for h in range(2):
             at = h * HALF + j * PART
             tall = jnp.concatenate([g[:, at : at + 128], g[:, at + 128 : at + 256]], axis=0)
             picked = jnp.dot(wide, tall, preferred_element_type=F32)
             tx[j, h * NZ : (h + 1) * NZ] = (picked * scale).astype(BF16).reshape(NZ, 16, 128)
 
+    pack(0)
     pl.semaphore_wait(barrier, 2 * (NZ - 1) + (NX - 1) + (2 * NY - 1))
 
-    for j in range(NJ if DISPATCH else 0):
+    for j in range(NJ):
+        if j > 0:
+            pack(j)
         rx_same[j, 0] = tx[j, c * NZ + z]
         for k in far_first:
             to = (z + k) % NZ
@@ -146,15 +134,30 @@
                 device_id_type=MESH,
             ).start()
 
-    for q in range(NX):
-        pltpu.make_async_remote_copy(
-            src_ref=w_hbm.at[0, :, pl.ds(pl.multiple_of(q * 1024 + (1 - c) * HALF, HALF), HALF)],
-            dst_ref=wbuf.at[1, q],
-            send_sem=wr_sem.at[0],
-            recv_sem=wr_sem.at[1],
-            device_id={"dp": partner},
-            device_id_type=MESH,
-        ).start()
+    cp_eo = fetch(1, eo_hbm, eo)
+    cp_tok = fetch(2, tok_hbm, tok)
+    cp_gate = fetch(3, gate_hbm.at[0], gate)
+    cp_up = fetch(4, up_hbm.at[0], up)
+
+    def weight(core, q, j):
+        return w_hbm.at[0, :, pl.ds(pl.multiple_of(q * 1024 + core * HALF + j * PART, PART), PART)]
+
+    for j in range(NJ):
+        for q in range(NX):
+            pltpu.make_async_copy(
+                weight(c, q, j), wbuf.at[j, pl.ds(0, HID), pl.ds(q * PART, PART)], w_sem.at[j]
+            ).start()
+
+    for j in range(NJ):
+        for q in range(NX):
+            pltpu.make_async_remote_copy(
+                src_ref=weight(1 - c, q, j),
+                dst_ref=wbuf.at[j, pl.ds(HID, HID), pl.ds(q * PART, PART)],
+                send_sem=wr_sem.at[0, j],
+                recv_sem=wr_sem.at[1, j],
+                device_id={"dp": partner},
+                device_id_type=MESH,
+            ).start()
 
     cp_eo.wait()
     parts = [jnp.zeros((128, 128), F32) for _ in range(2)]
@@ -167,7 +170,7 @@
     score = [jnp.sum(parts[k].T, axis=0, keepdims=True) for k in range(2)]
     sub = lax.broadcasted_iota(jnp.int32, (8, 128), 0)
     sc_tx[...] = jnp.where(sub == 0, score[0], jnp.where(sub == 1, score[1], 0.0))
-    for k in range(1, NX if ROUTER else 1):
+    for k in range(1, NX):
         pltpu.make_async_remote_copy(
             src_ref=sc_tx,
             dst_ref=sc_rx.at[k - 1],
@@ -187,73 +190,65 @@
         fac_u[:, part] = a * sigma
         fac_g[:, part] = b * sigma * (1.0 + a * (1.0 - sigma))
 
-    def place(ch, first, second):
-        if ch == 0:
-            return xs[first] * 4 + ys[second]
-        return xs[second] * 4 + ys[first]
-
-    def side_of(ch):
-        return c if ch == 0 else 1 - c
-
-    def push(ch, j, first, second, along_first, way, part, slot):
-        if not GATHER:
-            return
-        axis_x = along_first == (ch == 0)
-        if axis_x:
+    def place(o, first, second):
+        if o == 0:
+            return ys[second] * NX + xs[first]
+        return ys[first] * NX + xs[second]
+
+    def block(o, ch, j, first, second, half):
+        core = c if ch == 0 else 1 - c
+        some = pl.ds(0, 128) if half is None else pl.ds(half * 64, 64)
+        return rows.at[
+            j, place(o, first, second), o, some, pl.ds(pl.multiple_of(core * 128, 128), 128)
+        ]
+
+    def push(o, ch, j, first, second, along_first, way, half, slot):
+        if along_first == (o == 0):
             where = {"tensor": xs[way]}
         else:
             where = {"dp": ys[way] * 2 + c}
-        ref = rows.at[j, place(ch, first, second), side_of(ch)]
-        if part is not None:
-            ref = ref.at[pl.ds(part * 64, 64)]
+        ref = block(o, ch, j, first, second, half)
         pltpu.make_async_remote_copy(
             src_ref=ref,
             dst_ref=ref,
             send_sem=a_send.at[j],
-            recv_sem=a_recv.at[ch, j, slot],
+            recv_sem=a_recv.at[o, ch, j, slot],
             device_id=where,
             device_id_type=MESH,
         ).start()
 
-    def arrived(ch, j, first, second, part, slot):
-        if not GATHER:
-            return
-        ref = rows.at[j, place(ch, first, second), side_of(ch)]
-        if part is not None:
-            ref = ref.at[pl.ds(part * 64, 64)]
-        pltpu.make_async_copy(ref, ref, a_recv.at[ch, j, slot]).wait()
-
-    def spread(ch, j, first):
-        push(ch, j, first, OWN, False, PLUS, None, 4 + 4 * first)
-        push(ch, j, first, OWN, False, MINUS, None, 5 + 4 * first)
-
-    def step_a(ch, j):
-        push(ch, j, OWN, OWN, True, PLUS, None, 0)
-        push(ch, j, OWN, OWN, True, MINUS, None, 1)
-        spread(ch, j, OWN)
-
-    def step_b(ch, j):
-        arrived(ch, j, MINUS, OWN, None, 0)
-        push(ch, j, MINUS, OWN, True, PLUS, 0, 2)
-        spread(ch, j, MINUS)
-        arrived(ch, j, PLUS, OWN, None, 1)
-        push(ch, j, PLUS, OWN, True, MINUS, 1, 3)
-        spread(ch, j, PLUS)
-
-    def step_c(ch, j):
-        arrived(ch, j, OPP, OWN, 0, 2)
-        arrived(ch, j, OPP, OWN, 1, 3)
-        spread(ch, j, OPP)
-
-    def step_d(ch, j, first):
-        arrived(ch, j, first, MINUS, None, 4 + 4 * first)
-        push(ch, j, first, MINUS, False, PLUS, 0, 6 + 4 * first)
-        arrived(ch, j, first, PLUS, None, 5 + 4 * first)
-        push(ch, j, first, PLUS, False, MINUS, 1, 7 + 4 * first)
-
-    def step_e(ch, j, first):
-        arrived(ch, j, first, OPP, 0, 6 + 4 * first)
-        arrived(ch, j, first, OPP, 1, 7 + 4 * first)
+    def arrived(o, ch, j, first, second, half, slot):
+        ref = block(o, ch, j, first, second, half)
+        pltpu.make_async_copy(ref, ref, a_recv.at[o, ch, j, slot]).wait()
+
+    def spread(o, ch, j, first):
+        push(o, ch, j, first, OWN, False, PLUS, None, 4 + 4 * first)
+        push(o, ch, j, first, OWN, False, MINUS, None, 5 + 4 * first)
+
+    def step_a(o, ch, j):
+        push(o, ch, j, OWN, OWN, True, PLUS, None, 0)
+        push(o, ch, j, OWN, OWN, True, MINUS, None, 1)
+
+    def step_b(o, ch, j):
+        arrived(o, ch, j, MINUS, OWN, None, 0)
+        push(o, ch, j, MINUS, OWN, True, PLUS, 0, 2)
+        arrived(o, ch, j, PLUS, OWN, None, 1)
+        push(o, ch, j, PLUS, OWN, True, MINUS, 1, 3)
+
+    def step_c(o, ch, j):
+        arrived(o, ch, j, OPP, OWN, 0, 2)
+        arrived(o, ch, j, OPP, OWN, 1, 3)
+        spread(o, ch, j, OPP)
+
+    def step_d(o, ch, j, first):
+        arrived(o, ch, j, first, MINUS, None, 4 + 4 * first)
+        push(o, ch, j, first, MINUS, False, PLUS, 0, 6 + 4 * first)
+        arrived(o, ch, j, first, PLUS, None, 5 + 4 * first)
+        push(o, ch, j, first, PLUS, False, MINUS, 1, 7 + 4 * first)
+
+    def step_e(o, ch, j, first):
+        arrived(o, ch, j, first, OPP, 0, 6 + 4 * first)
+        arrived(o, ch, j, first, OPP, 1, 7 + 4 * first)
 
     out_row = lax.broadcasted_iota(jnp.int32, (256, 256), 0)
     in_row = lax.broadcasted_iota(jnp.int32, (256, 256), 1)
@@ -261,35 +256,47 @@
     want = src * 16 + (out_row // 128) * 8 + ((out_row // 32) % 4) * 2 + out_row % 2
     perm = (in_row == want).astype(BF16)
 
-    def unpack(ch, j):
-        if DISPATCH:
-            got = (rx_same.at[j, pl.ds(1, 15)], rx_cross.at[j])[ch]
-            pltpu.make_async_copy(got, got, z_recv.at[j, ch]).wait()
+    def unpacked(t):
+        ch, j = t % 2, t // 2
+        got = (rx_same.at[j, pl.ds(1, 15)], rx_cross.at[j])[ch]
+        pltpu.make_async_copy(got, got, z_recv.at[j, ch]).wait()
         packets = (rx_same, rx_cross)[ch][j].reshape(256, 128)
-        out = jnp.dot(perm, packets, preferred_element_type=F32).astype(BF16)
-        for f in range(2):
-            rows[j, place(ch, OWN, OWN), side_of(ch), :, f * 128 : (f + 1) * 128] = out[f * 128 : (f + 1) * 128]
-        step_a(ch, j)
+        out = jnp.dot(perm, packets, preferred_element_type=F32)
+        for o in range(2):
+            ref = block(o, ch, j, OWN, OWN, None)
+            ref[...] = out[o * 128 : (o + 1) * 128].T.astype(BF16)
+            step_a(o, ch, j)
+        for o in range(2):
+            spread(o, ch, j, OWN)
+
+    def near(t):
+        for o in range(2):
+            step_b(o, t % 2, t // 2)
+        for o in range(2):
+            spread(o, t % 2, t // 2, MINUS)
+            spread(o, t % 2, t // 2, PLUS)
+
+    def across(t):
+        for o in range(2):
+            step_c(o, t % 2, t // 2)
+
+    def onward(t, first):
+        for o in range(2):
+            step_d(o, t % 2, t // 2, first)
 
     def matmul(j, rel):
-        if not MATMUL:
+        for ch in range(2):
+            step_e(1, ch, j, rel)
+            if rel == OPP:
+                for first in range(4):
+                    step_e(0, ch, j, first)
+        cols = rows[j, pl.ds(ys[rel] * NX, NX)].reshape(NX * PART, 2 * ROWS)
+        total = jnp.dot(wbuf[j], cols, preferred_element_type=F32)
+        if j == 0:
+            p_own[rel] = total[0:HID]
+            p_tx[rel] = total[HID : 2 * HID]
             return
-        total = [None, None]
-        for q in range(NX):
-            block = rows[j, q * 4 + ys[rel]].reshape(2 * ROWS, PART)
-            for side in (0, 1):
-                term = lax.dot_general(
-                    wbuf[side, q, :, j * PART : (j + 1) * PART],
-                    block,
-                    (((1,), (1,)), ((), ())),
-                    preferred_element_type=F32,
-                )
-                total[side] = term if total[side] is None else total[side] + term
-        if j == 0:
-            p_own[rel] = total[0]
-            p_tx[rel] = total[1]
-            return
-        p_tx[rel] = p_tx[rel] + total[1]
+        p_tx[rel] = p_tx[rel] + total[HID : 2 * HID]
         pltpu.make_async_remote_copy(
             src_ref=p_tx.at[rel],
             dst_ref=p_rx.at[rel],
@@ -298,11 +305,9 @@
             device_id={"dp": partner},
             device_id_type=MESH,
         ).start()
-        p_own[rel] = p_own[rel] + total[0]
+        p_own[rel] = p_own[rel] + total[0:HID]
 
     def finish(rel):
-        if not MATMUL:
-            return
         pltpu.make_async_copy(p_rx.at[rel], p_rx.at[rel], p_recv.at[rel]).wait()
         hidden = p_own[rel] + p_rx[rel]
         at = pl.ds(pl.multiple_of(ys[rel] * 256, 256), 256)
@@ -310,8 +315,6 @@
         gg_ref[0, :, at] = (hidden * fac_g[:, at]).astype(BF16)
 
     def router_a():
-        if not ROUTER:
-            return
         for k in range(1, NX):
             pltpu.make_async_copy(sc_rx.at[k - 1], sc_rx.at[k - 1], sc_recv.at[k - 1]).wait()
         total = sc_tx[...] + sc_rx[0] + sc_rx[1] + sc_rx[2]
@@ -329,6 +332,8 @@
         term = terms[0:16] + terms[16:32] + terms[32:48]
         for p in range(16):
             rt[p] = term[(p // 8) * 8 : (p // 8) * 8 + 8, (p % 8) * 128 : (p % 8) * 128 + 128]
+
+    def router_e():
         for k in range(1, NZ):
             to = (z + k) % NZ
             pltpu.make_async_remote_copy(
@@ -341,8 +346,6 @@
             ).start()
 
     def router_b():
-        if not ROUTER:
-            return
         pltpu.make_async_copy(r1, r1, r_recv.at[0]).wait()
         total = rt[z]
         for k in range(NZ - 1):
@@ -359,8 +362,6 @@
             ).start()
 
     def router_c():
-        if not ROUTER:
-            return
         pltpu.make_async_copy(r2.at[pl.ds(0, 7)], r2.at[pl.ds(0, 7)], r_recv.at[1]).wait()
         total = r2[0]
         for k in range(1, 2 * NY):
@@ -377,105 +378,76 @@
             ).start()
 
     def router_d():
-        if not ROUTER:
-            return
         pltpu.make_async_copy(r3.at[pl.ds(0, 15)], r3.at[pl.ds(0, 15)], r_recv.at[2]).wait()
         for p in range(16):
             rg_ref[(p // 8) * 8 : (p // 8) * 8 + 8, (p % 8) * 128 : (p % 8) * 128 + 128] = r3[p]
 
-    def unpacked(t):
-        unpack(t % 2, t // 2)
-
-    def near(t):
-        step_b(t % 2, t // 2)
-
-    def across(t):
-        step_c(t % 2, t // 2)
-
-    def onward(t, first):
-        step_d(t % 2, t // 2, first)
-
-    def last(t):
-        for first in range(4):
-            step_e(t % 2, t // 2, first)
-
+    def weights_here():
+        for j in range(NJ):
+            own, other = wbuf.at[j, pl.ds(0, HID)], wbuf.at[j, pl.ds(HID, HID)]
+            pltpu.make_async_copy(own, own, w_sem.at[j]).wait()
+            pltpu.make_async_copy(other, other, wr_sem.at[1, j]).wait()
+
+    router_a()
+    router_e()
     unpacked(0)
-    router_a()
     unpacked(1)
     near(0)
     onward(0, OWN)
     unpacked(2)
-    across(0)
     near(1)
     onward(1, OWN)
+    across(0)
+    onward(0, MINUS)
+    onward(0, PLUS)
     unpacked(3)
-    onward(0, MINUS)
-    across(1)
     near(2)
     onward(2, OWN)
-    onward(0, PLUS)
+    across(1)
+    onward(1, MINUS)
+    onward(1, PLUS)
     router_b()
     near(3)
-    onward(1, MINUS)
     onward(3, OWN)
     across(2)
+    onward(2, MINUS)
+    onward(2, PLUS)
     onward(0, OPP)
+    onward(1, OPP)
     across(3)
-    onward(1, PLUS)
-    onward(2, MINUS)
-    onward(1, OPP)
     onward(3, MINUS)
-    pltpu.make_async_copy(wbuf.at[0], wbuf.at[0], w_sem.at[0]).wait()
-    pltpu.make_async_copy(wbuf.at[1], wbuf.at[1], wr_sem.at[1]).wait()
-    step_e(1, 0, OWN)
+    onward(3, PLUS)
+    router_c()
+    weights_here()
     matmul(0, OWN)
-    router_c()
-    onward(2, PLUS)
-    step_e(1, 0, MINUS)
     matmul(0, MINUS)
-    onward(3, PLUS)
-    step_e(1, 0, PLUS)
+    onward(2, OPP)
     matmul(0, PLUS)
-    onward(2, OPP)
-    step_e(1, 0, OPP)
-    for first in range(4):
-        step_e(0, 0, first)
     matmul(0, OPP)
     onward(3, OPP)
-    step_e(1, 1, OWN)
     matmul(1, OWN)
-    step_e(1, 1, MINUS)
     matmul(1, MINUS)
-    step_e(1, 1, PLUS)
     matmul(1, PLUS)
-    router_d()
     finish(OWN)
-    for first in range(4):
-        step_e(0, 1, first)
-    step_e(1, 1, OPP)
     matmul(1, OPP)
     finish(MINUS)
     finish(PLUS)
-    if not ROUTER:
-        cp_tok.wait()
-
+    router_d()
     for j in range(NJ):
-        if DISPATCH:
-            pltpu.make_async_copy(tx.at[j, pl.ds(0, 31)], tx.at[j, pl.ds(0, 31)], z_send.at[j]).wait()
-        if GATHER:
-            sent = rows.at[j, pl.ds(0, 15)]
-            pltpu.make_async_copy(sent, sent, a_send.at[j]).wait()
-    if ROUTER:
-        for k in range(NX - 1):
-            pltpu.make_async_copy(sc_tx, sc_tx, sc_send.at[k]).wait()
-        pltpu.make_async_copy(r1, r1, r_send.at[0]).wait()
-        pltpu.make_async_copy(r2.at[pl.ds(0, 7)], r2.at[pl.ds(0, 7)], r_send.at[1]).wait()
-        pltpu.make_async_copy(r1, r1, r_send.at[2]).wait()
-    pltpu.make_async_copy(wbuf.at[1], wbuf.at[1], wr_sem.at[0]).wait()
+        pltpu.make_async_copy(tx.at[j, pl.ds(0, 31)], tx.at[j, pl.ds(0, 31)], z_send.at[j]).wait()
+        sent = rows.at[j, pl.ds(0, 15)]
+        pltpu.make_async_copy(sent, sent, a_send.at[j]).wait()
+    for k in range(NX - 1):
+        pltpu.make_async_copy(sc_tx, sc_tx, sc_send.at[k]).wait()
+    pltpu.make_async_copy(r1, r1, r_send.at[0]).wait()
+    pltpu.make_async_copy(r2.at[pl.ds(0, 7)], r2.at[pl.ds(0, 7)], r_send.at[1]).wait()
+    pltpu.make_async_copy(r1, r1, r_send.at[2]).wait()
+    for j in range(NJ):
+        other = wbuf.at[j, pl.ds(HID, HID)]
+        pltpu.make_async_copy(other, other, wr_sem.at[0, j]).wait()
     finish(OPP)
-    if MATMUL:
-        for rel in range(NY):
-            pltpu.make_async_copy(p_tx.at[rel], p_tx.at[rel], p_send.at[rel]).wait()
+    for rel in range(NY):
+        pltpu.make_async_copy(p_tx.at[rel], p_tx.at[rel], p_send.at[rel]).wait()
 
 
 def body(
@@ -513,13 +485,13 @@
             pltpu.VMEM((2, 128), jnp.int32),
             pltpu.VMEM((2, 128), jnp.int32),
             pltpu.VMEM((2, 128), jnp.int32),
-            pltpu.VMEM((2, NX, HID, HALF), BF16),
+            pltpu.VMEM((NJ, 2 * HID, NX * PART), BF16),
             pltpu.VMEM((HID, slots), F32),
             pltpu.VMEM((HID, slots), F32),
             pltpu.VMEM((NJ, 2 * NZ, 16, 128), BF16),
             pltpu.VMEM((NJ, NZ, 16, 128), BF16),
             pltpu.VMEM((NJ, NZ, 16, 128), BF16),
-            pltpu.VMEM((NJ, NX * NY, 2, ROWS, PART), BF16),
+            pltpu.VMEM((NJ, NY * NX, 2, PART // 2, 2 * ROWS), BF16),
             pltpu.VMEM((NY, HID, 2 * ROWS), F32),
             pltpu.VMEM((NY, HID, 2 * ROWS), F32),
             pltpu.VMEM((NY, HID, 2 * ROWS), F32),
@@ -530,12 +502,12 @@
             pltpu.VMEM((2 * NY, 8, 128), F32),
             pltpu.VMEM((NZ, 8, 128), F32),
             dma((9,)),
-            dma((1,)),
-            dma((2,)),
+            dma((NJ,)),
+            dma((2, NJ)),
             dma((NJ,)),
             dma((NJ, 2)),
             dma((NJ,)),
-            dma((2, NJ, 20)),
+            dma((2, 2, NJ, 20)),
             dma((NY,)),
             dma((NY,)),
             dma((NX - 1,)),

time: 62 us -> 59.4 us (0.958)
  Pallas kernels: 59.1 us -> 56.4 us
    pallas_call x1, Pallas kernels: 59.1 us -> 56.4 us  [body(): pl.pallas_call(kernel, out_shape=(jax.ShapeDtypeStruct((1, HID, slots), B...]
where the time goes in v3:
time: 59.4 us; the launch traced here: 59.2 us
  Pallas kernels  56.4 us (95%)
  local copies, waits for them, and re-layouts  2.17 us (4%)
  between operations  0.64 us (1%)
    pallas_call x1, Pallas kernels, body(): pl.pallas_call(kernel, out_shape=(jax.ShapeDtypeStruct((1, HID, slots), B...  56.4 us
    unnamed x3, local copies, waits for them, and re-layouts  2.17 us

profile of v3, /device:TPU:1, one launch (start us, length us, event | category | flops | bytes accessed | tf_op | source)
XLA Modules:
  0.0 59.2 jit_solution(15826483966770055586)
XLA Ops:
  0.6 56.4 %shard_map.121 = (bf16[1,224,1024]{2,1,0:T(8,128)(2,1)S(1)}, bf16[1,224,1024]{2,1,0:T(8,128)(2,1)S(1)}, f32[16,1024]{1,0:T(8,128)S(1)}) custom-call(bf16[128,1024]{1,0:T(8,128)(2,1)} %g_hbm.1, bf16[128,1024]{1,0:T(8,128)(2,1)} %tok_hbm.1, bf16[128,2,1024]{2,1,0:T(2,128)(2,1)} %eo_hbm.1, bf16[1,224,1024]{2,1,0:T(8,128)(2,1)} %bitcast.10, ...), custom_call_target="tpu_custom_call" | custom-call | tf_op jit(solution)/shard_map/pallas_call | solution.py:469
  57.1 0.8 %copy.16 = bf16[1,1024,224]{1,2,0:T(8,128)(2,1)} copy(bf16[1,1024,224]{1,2,0:T(8,128)(2,1)S(1)} %bitcast.9) | data formatting | bytes 917504
  57.8 0.8 %copy.17 = bf16[1,1024,224]{1,2,0:T(8,128)(2,1)} copy(bf16[1,1024,224]{1,2,0:T(8,128)(2,1)S(1)} %bitcast.8) | data formatting | bytes 917504
  58.6 0.6 %copy.18 = f32[16,1024]{1,0:T(8,128)} copy(f32[16,1024]{1,0:T(8,128)S(1)} %get-tuple-element.14) | data formatting | bytes 131072

commit v4 on v3

--- a/solution.py
+++ b/solution.py
@@ -406,20 +406,20 @@
     across(1)
     onward(1, MINUS)
     onward(1, PLUS)
+    onward(0, OPP)
     router_b()
     near(3)
     onward(3, OWN)
     across(2)
     onward(2, MINUS)
     onward(2, PLUS)
-    onward(0, OPP)
     onward(1, OPP)
+    weights_here()
+    matmul(0, OWN)
     across(3)
     onward(3, MINUS)
     onward(3, PLUS)
     router_c()
-    weights_here()
-    matmul(0, OWN)
     matmul(0, MINUS)
     onward(2, OPP)
     matmul(0, PLUS)
@@ -433,6 +433,7 @@
     finish(MINUS)
     finish(PLUS)
     router_d()
+
     for j in range(NJ):
         pltpu.make_async_copy(tx.at[j, pl.ds(0, 31)], tx.at[j, pl.ds(0, 31)], z_send.at[j]).wait()
         sent = rows.at[j, pl.ds(0, 15)]

time: 59.4 us -> 59.4 us (level)
  no operation moved by 1% of the time
where the time goes in v4:
time: 59.4 us; the launch traced here: 59.2 us
  Pallas kernels  56.4 us (95%)
  local copies, waits for them, and re-layouts  2.17 us (4%)
  between operations  0.64 us (1%)
    pallas_call x1, Pallas kernels, body(): pl.pallas_call(kernel, out_shape=(jax.ShapeDtypeStruct((1, HID, slots), B...  56.4 us
    unnamed x3, local copies, waits for them, and re-layouts  2.17 us

profile of v4, /device:TPU:1, one launch (start us, length us, event | category | flops | bytes accessed | tf_op | source)
XLA Modules:
  0.0 59.2 jit_solution(8074912868619317677)
XLA Ops:
  0.6 56.4 %shard_map.121 = (bf16[1,224,1024]{2,1,0:T(8,128)(2,1)S(1)}, bf16[1,224,1024]{2,1,0:T(8,128)(2,1)S(1)}, f32[16,1024]{1,0:T(8,128)S(1)}) custom-call(bf16[128,1024]{1,0:T(8,128)(2,1)} %g_hbm.1, bf16[128,1024]{1,0:T(8,128)(2,1)} %tok_hbm.1, bf16[128,2,1024]{2,1,0:T(2,128)(2,1)} %eo_hbm.1, bf16[1,224,1024]{2,1,0:T(8,128)(2,1)} %bitcast.10, ...), custom_call_target="tpu_custom_call" | custom-call | tf_op jit(solution)/shard_map/pallas_call | solution.py:470
  57.1 0.8 %copy.16 = bf16[1,1024,224]{1,2,0:T(8,128)(2,1)} copy(bf16[1,1024,224]{1,2,0:T(8,128)(2,1)S(1)} %bitcast.9) | data formatting | bytes 917504
  57.8 0.8 %copy.17 = bf16[1,1024,224]{1,2,0:T(8,128)(2,1)} copy(bf16[1,1024,224]{1,2,0:T(8,128)(2,1)S(1)} %bitcast.8) | data formatting | bytes 917504
  58.6 0.6 %copy.18 = f32[16,1024]{1,0:T(8,128)} copy(f32[16,1024]{1,0:T(8,128)S(1)} %get-tuple-element.14) | data formatting | bytes 131072
